TPU v7x, 32 devices: a whole 2x2x4 slice. The times are simulated.
32 devices in a mesh: dp: 16 (over z, y, core), tensor: 2 (over x).
Axes of the slice: x: 2, y: 2, z: 4, core: 2. Of those that a mesh axis runs over, the one named last changes fastest.
Arguments:
- stream: bfloat16 [16, 1024, 1024], P('dp', 'tensor'), may hold values from -6 to 6
- norm_gain: float32 [1024], replicated, may hold values from 0.5 to 1.5
- proj_gate: bfloat16 [1024, 2048], P('dp', 'tensor'), may hold values from -0.1875 to 0.1875
- proj_input: bfloat16 [1024, 2048], P('dp', 'tensor'), may hold values from -0.1875 to 0.1875
- proj_state: bfloat16 [1024, 256], P('dp'), may hold values from -0.1875 to 0.1875
- proj_step: bfloat16 [1024, 32], P('dp', 'tensor'), may hold values from -0.1875 to 0.1875
- conv_input: float32 [4, 2048], P(None, 'tensor'), may hold values from -3 to 3
- conv_state: float32 [4, 256], replicated, may hold values from -3 to 3
- bias_input: float32 [2048], P('tensor'), may hold values from -0.5 to 0.5
- bias_state: float32 [256], replicated, may hold values from -0.5 to 0.5
- step_bias: float32 [32], P('tensor'), may hold values from -5 to -1
- decay_log: float32 [32], P('tensor'), may hold values from -3 to 1
- skip_gain: float32 [32], P('tensor'), may hold values from 0.5 to 1.5
- gate_gain: float32 [2048], P('tensor'), may hold values from 0.5 to 1.5
- proj_output: bfloat16 [2048, 1024], P('tensor', 'dp'), may hold values from -0.125 to 0.125
- cotangent: bfloat16 [16, 1024, 1024], P('dp', 'tensor'), may hold values from -6 to 6
Outputs:
- output: bfloat16 [16, 1024, 1024], P('dp', 'tensor')
- grad_stream: bfloat16 [16, 1024, 1024], P('dp', 'tensor')
- grad_norm_gain: float32 [1024], replicated
- grad_proj_gate: float32 [1024, 2048], P('dp', 'tensor')
- grad_proj_input: float32 [1024, 2048], P('dp', 'tensor')
- grad_proj_state: float32 [1024, 256], P('dp')
- grad_proj_step: float32 [1024, 32], P('dp', 'tensor')
- grad_conv_input: float32 [4, 2048], P(None, 'tensor')
- grad_conv_state: float32 [4, 256], replicated
- grad_bias_input: float32 [2048], P('tensor')
- grad_bias_state: float32 [256], replicated
- grad_step_bias: float32 [32], P('tensor')
- grad_decay_log: float32 [32], P('tensor')
- grad_skip_gain: float32 [32], P('tensor')
- grad_gate_gain: float32 [2048], P('tensor')
- grad_proj_output: float32 [2048, 1024], P('tensor', 'dp')
All inputs are finite; a program needn't handle non-finite values.
Results may differ from a plain program's by a relative error of at most 0.017.
Values may be sent and summed in bfloat16 or wider, within the bound.
A program may use at most 192 MiB of HBM per device.

v0:
```python
import jax
import jax.numpy as jnp
from jax import lax
from jax.sharding import PartitionSpec as P

SPAN = 256
DI = 2048


EPS = 1e-05
HIGH_ACCURACY = lax.Precision.HIGHEST


def causal(values, kernel):
    tap_count = kernel.shape[0]
    length = values.shape[1]
    padded = jnp.pad(values, ((0, 0), (tap_count - 1, 0), (0, 0)))
    summed = kernel[0] * padded[:, 0:length]
    for tap_index in range(1, tap_count):
        summed = summed + kernel[tap_index] * padded[:, tap_index : tap_index + length]
    return summed


def span_scan(signal, dt_step, log_rate, b_rows, c_rows):
    seq_count, length, head_count, head_dim = signal.shape
    blocks = length // SPAN
    sig_blk = (signal * dt_step[..., None]).reshape(seq_count, blocks, SPAN, head_count, head_dim)
    rate_blk = jnp.moveaxis(log_rate.reshape(seq_count, blocks, SPAN, head_count), 3, 2)
    b_blk = b_rows.reshape(seq_count, blocks, SPAN, -1)
    c_blk = c_rows.reshape(seq_count, blocks, SPAN, -1)
    cumulative = jnp.cumsum(rate_blk, axis=-1)
    row_pos = lax.broadcasted_iota(jnp.int32, (SPAN, SPAN), 0)
    col_pos = lax.broadcasted_iota(jnp.int32, (SPAN, SPAN), 1)
    gap_sum = cumulative[..., :, None] - cumulative[..., None, :]
    weights = jnp.exp(jnp.where(row_pos >= col_pos, gap_sum, -jnp.inf))
    scores = jnp.einsum("scqn,scrn->scqr", c_blk, b_blk, precision=HIGH_ACCURACY)
    blended = scores[:, :, None] * weights
    y_within = jnp.einsum("schqr,scrhp->scqhp", blended, sig_blk, precision=HIGH_ACCURACY)
    to_end = jnp.exp(cumulative[..., -1:] - cumulative)
    states = jnp.einsum("scrn,schr,scrhp->schnp", b_blk, to_end, sig_blk, precision=HIGH_ACCURACY)
    carried = jnp.exp(cumulative[..., -1])

    def advance(previous, inputs):
        span_state, factor = inputs
        return (factor[..., None, None] * previous + span_state, previous)

    initial = jnp.zeros(states.shape[:1] + states.shape[2:], states.dtype)
    _, entering = lax.scan(
        advance, initial, (jnp.moveaxis(states, 1, 0), jnp.moveaxis(carried, 1, 0))
    )
    entering = jnp.moveaxis(entering, 0, 1)
    y_across = jnp.einsum(
        "scqn,schq,schnp->scqhp", c_blk, jnp.exp(cumulative), entering, precision=HIGH_ACCURACY
    )
    return (y_within + y_across).reshape(seq_count, length, head_count, head_dim)


def mixer(
    gate_pre,
    input_pre,
    state_pre,
    step_pre,
    conv_input,
    conv_state,
    bias_input,
    bias_state,
    step_bias,
    decay_log,
    skip_gain,
):
    seq_count, length, channels = input_pre.shape
    head_count = step_pre.shape[-1]
    signal = jax.nn.silu(causal(input_pre, conv_input) + bias_input)
    state_in = jax.nn.silu(causal(state_pre, conv_state) + bias_state)
    half_width = state_in.shape[-1] // 2
    dt_step = jax.nn.softplus(step_pre + step_bias)
    log_rate = -jnp.exp(decay_log) * dt_step
    heads_sig = signal.reshape(seq_count, length, head_count, channels // head_count)
    scanned = span_scan(
        heads_sig, dt_step, log_rate, state_in[..., :half_width], state_in[..., half_width:]
    )
    scanned = scanned + skip_gain[:, None] * heads_sig
    return scanned.reshape(seq_count, length, channels) * jax.nn.silu(gate_pre)


def local(
    stream,
    norm_gain,
    proj_gate,
    proj_input,
    proj_state,
    proj_step,
    conv_input,
    conv_state,
    bias_input,
    bias_state,
    step_bias,
    decay_log,
    skip_gain,
    gate_gain,
    proj_output,
    cotangent,
):
    stream_f = stream.astype(jnp.float32)
    inv_rms = lax.rsqrt(jnp.mean(stream_f * stream_f, axis=-1, keepdims=True) + EPS)
    normed = stream_f * inv_rms
    hidden_values = (normed * norm_gain).astype(jnp.bfloat16)
    complete_hidden = lax.all_gather(hidden_values, "tensor", axis=1, tiled=True)
    gate_w, input_w, state_w, step_w, out_w = (
        lax.all_gather(proj_gate, "dp", axis=0, tiled=True),
        lax.all_gather(proj_input, "dp", axis=0, tiled=True),
        lax.all_gather(proj_state, "dp", axis=0, tiled=True),
        lax.all_gather(proj_step, "dp", axis=0, tiled=True),
        lax.all_gather(proj_output, "dp", axis=1, tiled=True),
    )

    def project(weight_matrix):
        return jnp.einsum(
            "nbp,pr->nbr", complete_hidden, weight_matrix, preferred_element_type=jnp.float32
        )

    mixed, pull_back = jax.vjp(
        mixer,
        project(gate_w),
        project(input_w),
        project(state_w),
        project(step_w),
        conv_input,
        conv_state,
        bias_input,
        bias_state,
        step_bias,
        decay_log,
        skip_gain,
    )
    square_all = lax.psum(jnp.sum(mixed * mixed, axis=-1), "tensor")
    scale = lax.rsqrt(square_all / DI + EPS)[..., None]
    gated = (mixed * scale * gate_gain).astype(jnp.bfloat16)
    partial_out = jnp.einsum("slc,ce->sle", gated, out_w, preferred_element_type=jnp.float32)
    branch_out = lax.psum_scatter(
        partial_out.astype(jnp.bfloat16), "tensor", scatter_dimension=1, tiled=True
    ).astype(jnp.float32)
    output = (stream_f + branch_out).astype(jnp.bfloat16)
    cot_full = lax.all_gather(cotangent, "tensor", axis=1, tiled=True)
    gate_batch, input_batch, state_batch, step_batch, out_b = (
        lax.all_gather(proj_gate, "dp", axis=0, tiled=True),
        lax.all_gather(proj_input, "dp", axis=0, tiled=True),
        lax.all_gather(proj_state, "dp", axis=0, tiled=True),
        lax.all_gather(proj_step, "dp", axis=0, tiled=True),
        lax.all_gather(proj_output, "dp", axis=1, tiled=True),
    )
    grad_gated = jnp.einsum("sle,ce->slc", cot_full, out_b, preferred_element_type=jnp.float32)
    grad_out_w = jnp.einsum("slc,sle->ce", gated, cot_full, preferred_element_type=jnp.float32)
    weighted = grad_gated * gate_gain
    grad_gate_gain = jnp.sum(grad_gated * mixed * scale, axis=(0, 1))
    inner_dot = lax.psum(jnp.sum(weighted * mixed, axis=-1), "tensor")
    grad_mixed = scale * weighted - mixed * scale * scale * scale * (inner_dot / DI)[..., None]
    pieces = pull_back(grad_mixed)
    state_total, conv_state_g, bias_state_g = (
        lax.psum(pieces[2].astype(jnp.bfloat16), "tensor").astype(jnp.float32),
        lax.psum(pieces[5].astype(jnp.bfloat16), "tensor").astype(jnp.float32),
        lax.psum(pieces[7].astype(jnp.bfloat16), "tensor").astype(jnp.float32),
    )
    gradient_gate_preactive = pieces[0].astype(jnp.bfloat16)
    gradient_input_preactive = pieces[1].astype(jnp.bfloat16)
    grad_state_pre = state_total.astype(jnp.bfloat16)
    gradient_step_preactive = pieces[3].astype(jnp.bfloat16)
    back_terms = jnp.einsum(
        "tzi,ni->tzn", gradient_gate_preactive, gate_batch, preferred_element_type=jnp.float32
    )
    back_terms = back_terms + jnp.einsum(
        "tzi,ni->tzn", gradient_input_preactive, input_batch, preferred_element_type=jnp.float32
    )
    back_terms = back_terms + jnp.einsum(
        "tzi,ni->tzn", gradient_step_preactive, step_batch, preferred_element_type=jnp.float32
    )
    own_rows = stream.shape[1]
    row_start = lax.axis_index("tensor") * own_rows
    state_row_values = lax.dynamic_slice_in_dim(grad_state_pre, row_start, own_rows, 1)
    grad_hidden = lax.psum_scatter(
        back_terms.astype(jnp.bfloat16), "tensor", scatter_dimension=1, tiled=True
    ).astype(jnp.float32)
    grad_hidden = grad_hidden + jnp.einsum(
        "tzi,ni->tzn", state_row_values, state_batch, preferred_element_type=jnp.float32
    )

    def weight_grad(gradient_preactive):
        return jnp.einsum(
            "gek,gew->kw", complete_hidden, gradient_preactive, preferred_element_type=jnp.float32
        )

    shard_gate, shard_input, shard_state, shard_step, shard_out = (
        lax.psum_scatter(
            weight_grad(gradient_gate_preactive).astype(jnp.bfloat16),
            "dp",
            scatter_dimension=0,
            tiled=True,
        ).astype(jnp.float32),
        lax.psum_scatter(
            weight_grad(gradient_input_preactive).astype(jnp.bfloat16),
            "dp",
            scatter_dimension=0,
            tiled=True,
        ).astype(jnp.float32),
        lax.psum_scatter(
            weight_grad(grad_state_pre).astype(jnp.bfloat16), "dp", scatter_dimension=0, tiled=True
        ).astype(jnp.float32),
        lax.psum_scatter(
            weight_grad(gradient_step_preactive).astype(jnp.bfloat16),
            "dp",
            scatter_dimension=0,
            tiled=True,
        ).astype(jnp.float32),
        lax.psum_scatter(
            grad_out_w.astype(jnp.bfloat16), "dp", scatter_dimension=1, tiled=True
        ).astype(jnp.float32),
    )
    weighted_h = grad_hidden * norm_gain
    norm_dot = jnp.mean(weighted_h * normed, axis=-1, keepdims=True)
    grad_stream = (
        cotangent.astype(jnp.float32) + inv_rms * (weighted_h - normed * norm_dot)
    ).astype(jnp.bfloat16)
    norm_part = jnp.sum(grad_hidden * normed, axis=(0, 1))
    conv_in_g, conv_st_g, bias_in_g, bias_st_g, step_bias_g, decay_g, skip_g, gate_gain_g = (
        lax.psum(
            (
                pieces[4],
                conv_state_g,
                pieces[6],
                bias_state_g,
                pieces[8],
                pieces[9],
                pieces[10],
                grad_gate_gain,
            ),
            "dp",
        )
    )
    norm_total = lax.psum(norm_part, ("dp", "tensor"))
    return (
        output,
        grad_stream,
        norm_total,
        shard_gate,
        shard_input,
        shard_state,
        shard_step,
        conv_in_g,
        conv_st_g,
        bias_in_g,
        bias_st_g,
        step_bias_g,
        decay_g,
        skip_g,
        gate_gain_g,
        shard_out,
    )


def solution(mesh):
    placed = (
        P("dp", "tensor", None),
        P(),
        P("dp", "tensor"),
        P("dp", "tensor"),
        P("dp", None),
        P("dp", "tensor"),
        P(None, "tensor"),
        P(),
        P("tensor"),
        P(),
        P("tensor"),
        P("tensor"),
        P("tensor"),
        P("tensor"),
        P("tensor", "dp"),
        P("dp", "tensor", None),
    )
    return jax.shard_map(
        local,
        mesh=mesh,
        in_specs=placed,
        out_specs=(
            P("dp", "tensor", None),
            P("dp", "tensor", None),
            P(),
            P("dp", "tensor"),
            P("dp", "tensor"),
            P("dp", None),
            P("dp", "tensor"),
            P(None, "tensor"),
            P(),
            P("tensor"),
            P(),
            P("tensor"),
            P("tensor"),
            P("tensor"),
            P("tensor"),
            P("tensor", "dp"),
        ),
        check_vma=False,
    )
```

profile of v0, /device:TPU:0, one launch (start us, length us, event | category | flops | bytes accessed | tf_op | source)
XLA Modules:
  0.0 810.5 jit_solution(10543825946357402901)
XLA Ops:
  15.1 23.3 %all-gather = bf16[16,64,16]{1,2,0:T(8,128)(2,1)S(1)} all-gather(bf16[1,64,16]{1,2,0:T(8,128)(2,1)S(1)} %bitcast.420), channel_id=1, replica_groups=mesh['dp'=16,'tensor'=2] {'dp'}, dimensions={0}, use_global_device_ids=true | all-gather | bytes 34816 | tf_op jit(solution)/shard_map/all_gather | solution.py:113
  38.5 18.9 %all_gather.29 = bf16[1024,256]{1,0:T(8,128)(2,1)S(1)} all-gather(bf16[64,256]{1,0:T(8,128)(2,1)S(1)} %copy-done.44), channel_id=1, replica_groups=mesh['dp'=16,'tensor'=2] {'dp'}, dimensions={0}, use_global_device_ids=true | all-gather | bytes 557056 | tf_op jit(solution)/shard_map/all_gather | solution.py:112
  71.2 19.7 %all-gather.9.cloned.1.call-done = bf16[1024,1024]{1,0:T(8,128)(2,1)} async-done(((bf16[64,1024]{1,0:T(8,128)(2,1)}), bf16[1024,1024]{1,0:T(8,128)(2,1)}) %all-gather.9.cloned.1.call-update) | async-done | bytes 2097168 | tf_op jit(solution)/shard_map/all_gather | solution.py:111
  100.1 7.3 reshape.779
  107.4 8.1 %copy.174 = f32[4,256,16,64]{1,3,2,0:T(8,128)} copy(f32[4,256,16,64]{3,2,1,0:T(8,128)} %reshape.779) | data formatting | bytes 8388608 | tf_op jit(solution)/shard_map/jvp()/reshape | solution.py:78
  115.5 7.7 fusion.115
  125.7 20.3 %while.34 = (s32[]{:T(128)}, f32[1,16,128,64]{3,2,1,0:T(8,128)S(1)}, f32[4,1,16,128,64]{4,3,2,1,0:T(8,128)}, f32[4,1,16,1,1]{2,4,3,1,0:T(1,128)}, f32[4,1,16]{2,...) while((s32[]{:T(128)}, f32[1,16,128,64]{3,2,1,0:T(8,128)S(1)}, ...), condition=%wide.region_4.5_spmd.clone, body=%wide.region_3.4_spmd.clone.sunk | while | flops 524291 | bytes 5243768 | solution.py:48
  151.4 8.7 %fusion.40 = f32[4,16,64,256]{3,2,1,0:T(8,128)S(1)} fusion(f32[4,256,128,1]{2,1,3,0:T(8,128)S(1)} %bitcast.365, f32[4,1,16,128,64]{4,3,2,1,0:T(8,128)} %get-tuple-element.522), kind=kOutput, calls=%fused_computation.67 | convolution fusion | flops 1610612736 | bytes 6815744 | tf_op jit(solution)/shard_map/jvp(scqn,schq,schnp->scqhp)/dot_general | solution.py:52
  162.1 19.9 %bitcast_add_fusion.3 = f32[1,4,256,16,64]{2,4,3,1,0:T(8,128)} fusion(f32[4,16,64,256]{3,2,1,0:T(8,128)S(1)} %fusion.40, f32[4,256,16]{1,2,0:T(8,128)S(1)} %get-tuple-element.368, f32[4,16,256]{2,1,0:T(8,128)S(1)} %get-tuple-element.369, f32[4,256,256]{2,1,0:T(8,128)S(1)} %copy-done.22, pred[256,256]{1,0:T(8,128)(4,1)S(1)} %copy-done.34, ...), kind=kOutput, calls=%fused_computation.44 | convolution fusion | flops 3236954112 | bytes 13893632 | tf_op jit(solution)/shard_map/jvp(schqr,scrhp->scqhp)/dot_general | solution.py:38
  182.0 8.1 copy.231
  190.1 7.7 reshape.780
  197.8 11.5 %multiply_reduce_fusion.8 = (f32[1024]{0:T(1024)S(1)}, f32[1024,1024]{1,0:T(8,128)}, f32[1024,1024]{1,0:T(8,128)}) fusion(f32[1024,1024]{1,0:T(8,128)} %reshape.780, f32[1,1024,1024]{2,1,0:T(8,128)} %get-tuple-element.371, f32[1024]{0:T(1024)S(1)} %mul.592, bf16[1024,1024]{1,0:T(8,128)(2,1)} %all-gather.11.cloned.1.call-done, ...), kind=kOutput, calls=%fused_computation.81 | convolution fusion | flops 2161114112 | bytes 20979712 | tf_op jit(solution)/shard_map/nbp,pr->nbr/dot_general | solution.py:118
  214.3 8.6 %multiply_reduce_fusion.1 = (f32[1024]{0:T(1024)}, f32[1024]{0:T(1024)S(1)}, f32[1024,1024]{1,0:T(8,128)}) fusion(f32[1024,1024]{1,0:T(8,128)} %get-tuple-element.367, f32[1024]{0:T(1024)S(1)} %bitcast.387, f32[1024]{0:T(1024)S(1)} %copy-done.47, bf16[1024,1024]{0,1:T(8,128)(2,1)} %all-gather.13.cloned.1.call-done, ...), kind=kOutput, calls=%fused_computation.71 | convolution fusion | flops 2153773056 | bytes 12599296 | tf_op jit(solution)/shard_map/sle,ce->slc/dot_general | solution.py:152
  227.8 9.2 %fusion.26 = (f32[1024]{0:T(1024)}, f32[1024,1024]{1,0:T(8,128)}) fusion(f32[1,1024,1024]{2,1,0:T(8,128)} %get-tuple-element.371, f32[1024,1024]{1,0:T(8,128)} %get-tuple-element.400, f32[1024]{0:T(1024)S(1)} %bitcast.392, f32[1024,1024]{1,0:T(8,128)} %get-tuple-element.367, f32[1024,1024]{1,0:T(8,128)} %get-tuple-element.401, f32[1024]{0:T(1024)S(1)} %copy-done.47, ...), kind=kLoop, calls=%fused_computation.46 | loop fusion | flops 18873344 | bytes 20987904 | tf_op jit(solution)/shard_map/transpose(jvp())/reduce_sum | solution.py:82
  260.0 14.4 %fusion.126 = f32[4,256,128]{2,1,0:T(8,128)} fusion(f32[4,1,16,128,64]{4,3,2,1,0:T(8,128)S(1)} %copy-done, f32[4,256,16,64]{1,0,3,2:T(4,128)S(1)} %copy-done.3, f32[4,256,16]{1,2,0:T(8,128)S(1)} %get-tuple-element.368), kind=kOutput, calls=%fused_computation.159 | convolution fusion | flops 1611661312 | bytes 6881280 | tf_op jit(solution)/shard_map/transpose(jvp(scqn,schq,schnp->scqhp))/dot_general | solution.py:52
  282.8 23.1 %while.35 = (s32[]{:T(128)}, f32[1,16,128,64]{3,2,1,0:T(8,128)S(1)}, f32[4,1,16,128,64]{4,3,2,1,0:T(8,128)}, f32[4,1,16]{2,1,0:T(1,128)}, f32[4,1,16,128,64]{3,4...) while((s32[]{:T(128)}, ...), condition=%wide.region_12.13_spmd.clone, body=%wide.region_10.12_spmd.clone.sunk | while | flops 786420 | bytes 5768152 | solution.py:48
  307.4 26.8 %fusion.9 = (f32[4,16,256]{2,1,0:T(8,128)}, f32[4,16,256]{2,1,0:T(8,128)}, f32[4,256,256]{2,1,0:T(8,128)S(1)}) fusion(f32[4,16,256]{2,1,0:T(8,128)S(1)} %copy-done.31, f32[4,256,256]{2,1,0:T(8,128)} %fusion.184, pred[256,256]{1,0:T(8,128)(4,1)} %iota_compare_fusion, f32[4,256,16,64]{1,3,2,0:T(8,128)} %copy.174, f32[4,256,16]{1,2,0:T(8,128)S(1)} %bitcast.374, ...), kind=kOutput, calls=%fused_computation.21 | convolution fusion | flops 3259727872 | bytes 10813440 | tf_op jit(solution)/shard_map/transpose(jvp(schqr,scrhp->scqhp))/dot_general | solution.py:38
  335.3 6.8 fusion.36
  347.3 15.3 %bitcast_add_fusion.2 = f32[1,4,256,16,64]{2,4,3,1,0:T(8,128)} fusion(f32[4,16,64,256]{3,2,1,0:T(8,128)S(1)} %get-tuple-element.403, f32[4,256,16]{1,2,0:T(8,128)S(1)} %exponential_bitcast_fusion, f32[4,16,256]{2,1,0:T(8,128)S(1)} %copy-done.32, f32[4,256,256]{2,1,0:T(8,128)S(1)} %copy-done.23, pred[256,256]{1,0:T(8,128)(4,1)S(1)} %copy-done.35, ...), kind=kOutput, calls=%fused_computation.43 | convolution fusion | flops 3235905536 | bytes 13828096 | tf_op jit(solution)/shard_map/transpose(jvp(schqr,scrhp->scqhp))/dot_general | solution.py:38
  369.3 9.9 %reduce-window.16 = f32[1,4,16,2,128]{4,2,3,1,0:T(8,128)S(1)} reduce-window(f32[1,4,16,2,128]{4,2,3,1,0:T(8,128)S(1)} %copy.200, f32[]{:T(128)} %constant.103.clone.1), window={size=1x1x1x1x128 pad=0_0x0_0x0_0x0_0x0_127}, to_apply=%region_17.18 | reduce-window | flops 2080768 | bytes 131076 | tf_op jit(solution)/shard_map/reduce-window.2
  390.0 20.8 %all-reduce.26.cloned.1.call-done = bf16[1,1024,256]{2,1,0:T(8,128)(2,1)} async-done(((bf16[1,1024,256]{2,1,0:T(8,128)(2,1)}), bf16[1,1024,256]{2,1,0:T(8,128)(2,1)}) %all-reduce.26.cloned.1.call-update) | async-done | bytes 524304 | tf_op jit(solution)/shard_map/psum | solution.py:160
  413.8 6.8 fusion.112
  428.5 8.1 %copy.232 = f32[1,4,256,16,64]{4,3,2,1,0:T(8,128)} copy(f32[1,4,256,16,64]{2,4,3,1,0:T(8,128)} %bitcast_add_fusion.2) | data formatting | bytes 8388608 | tf_op jit(solution)/shard_map/transpose(jvp())/reshape | solution.py:27
  436.6 7.6 reshape.781
  444.2 9.2 %fusion.22 = bf16[1024,1024]{1,0:T(8,128)(2,1)S(1)} fusion(f32[1024,1024]{1,0:T(8,128)} %get-tuple-element.400, f32[1024]{0:T(1024)S(1)} %bitcast.393, f32[1024,1024]{1,0:T(8,128)} %get-tuple-element.367, f32[1024,1024]{1,0:T(8,128)} %get-tuple-element.401, f32[1024]{0:T(1024)S(1)} %copy-done.48, f32[1024]{0:T(1024)S(1)} %bitcast.390, ...), kind=kLoop, calls=%fused_computation.36 | loop fusion | flops 25165824 | bytes 23085056 | tf_op jit(solution)/shard_map/convert_element_type | solution.py:164
  459.0 15.0 %multiply_reduce_fusion.4 = (f32[1024]{0:T(1024)S(1)}, f32[1024]{0:T(1024)S(1)}, f32[1024]{0:T(1024)S(1)}, f32[1024]{0:T(1024)S(1)}, f32[1024]{0:T(1024)S(1)}, /*index=5*/f32[1,1024,1024]{2,1,0:T(8,128)}) fusion(f32[1,1024,1024]{2,1,0:T(8,128)} %bitcast.353, f32[1024,1024]{1,0:T(8,128)} %copy-done.4, f32[1,1024,1024]{2,1,0:T(8,128)} %get-tuple-element.371, ...), kind=kLoop, calls=%fused_computation.74 | loop fusion | flops 22014976 | bytes 29384704 | tf_op jit(solution)/shard_map/transpose(jvp())/reduce_sum | solution.py:20
  513.3 61.0 %all-reduce.22 = (f32[4,1024]{1,0:T(4,128)}, f32[4,256]{1,0:T(4,128)}, f32[1024]{0:T(1024)}, f32[256]{0:T(256)}, f32[16]{0:T(128)}, /*index=5*/f32[16]{0:T(128)}, f32[16]{0:T(128)}, f32[1024]{0:T(1024)}) all-reduce(f32[4,1024]{1,0:T(4,128)S(1)} %pad_add_fusion.6, ...), channel_id=1, replica_groups=mesh['dp'=16,'tensor'=2] {'dp'}, use_global_device_ids=true, to_apply=%region_33.34 | all-reduce | flops 7472 | bytes 57216 | tf_op jit(solution)/shard_map/psum | solution.py:225
  577.0 17.7 %reduce-scatter.20.cloned.1.call-done = bf16[1024,64]{0,1:T(8,128)(2,1)} async-done(((bf16[1024,1024]{0,1:T(8,128)(2,1)}), bf16[1024,64]{0,1:T(8,128)(2,1)}) %reduce-scatter.20.cloned.1.call-update) | async-done | bytes 131088 | tf_op jit(solution)/shard_map/reduce_scatter | solution.py:214
  596.3 63.0 %reduce-scatter.14.cloned.1.call-done = bf16[64,1024]{1,0:T(8,128)(2,1)} async-done(((bf16[1024,1024]{1,0:T(8,128)(2,1)}), bf16[64,1024]{1,0:T(8,128)(2,1)}) %reduce-scatter.14.cloned.1.call-update) | async-done | bytes 131088 | tf_op jit(solution)/shard_map/reduce_scatter | solution.py:193
  660.9 62.7 %reduce-scatter.16.cloned.1.call-done = bf16[64,1024]{1,0:T(8,128)(2,1)} async-done(((bf16[1024,1024]{1,0:T(8,128)(2,1)}), bf16[64,1024]{1,0:T(8,128)(2,1)}) %reduce-scatter.16.cloned.1.call-update) | async-done | bytes 131088 | tf_op jit(solution)/shard_map/reduce_scatter | solution.py:199
  725.3 31.4 %reduce-scatter.12.cloned.1.call-done = bf16[1,512,1024]{2,1,0:T(8,128)(2,1)} async-done(((bf16[1,1024,1024]{2,1,0:T(8,128)(2,1)}), bf16[1,512,1024]{2,1,0:T(8,128)(2,1)}) %reduce-scatter.12.cloned.1.call-update) | async-done | bytes 1048592 | tf_op jit(solution)/shard_map/reduce_scatter | solution.py:180
  760.2 39.5 %psum.101 = f32[1024]{0:T(1024)} all-reduce(f32[1024]{0:T(1024)S(1)} %get-tuple-element.315), channel_id=1, replica_groups=mesh['dp'=16,'tensor'=2] {'dp','tensor'}, use_global_device_ids=true, to_apply=%region_24.25 | all-reduce | flops 1024 | bytes 8192 | tf_op jit(solution)/shard_map/psum | solution.py:239
  (332 shorter events, 220.4 us)
Async XLA Ops:
  7.2 31.2 %copy-start.44 = (bf16[64,256]{1,0:T(8,128)(2,1)S(1)}, bf16[64,256]{1,0:T(8,128)(2,1)}, u32[]{:S(2)}) copy-start(bf16[64,256]{1,0:T(8,128)(2,1)} %param.24) | copy-start | bytes 98308
  7.2 50.1 %copy-start.68 = (f32[16]{0:T(128)S(1)}, f32[16]{0:T(128)}, u32[]{:S(2)}) copy-start(f32[16]{0:T(128)} %param.30) | copy-start | bytes 196
  7.3 50.1 %all-gather.7.cloned.1.call-start = ((), (), s32[]{:S(2)}) async-start(), calls=%async_computation.7 | async-start | bytes 3145728 | tf_op jit(solution)/shard_map/all_gather | solution.py:108
  11.4 79.6 %all-gather.9.cloned.1.call-start = ((), (), s32[]{:S(2)}) async-start(), calls=%async_computation.8 | async-start | bytes 2228224 | tf_op jit(solution)/shard_map/all_gather | solution.py:111
  12.1 185.7 %all-gather.11.cloned.1.call-start = ((), (), s32[]{:S(2)}) async-start(), calls=%async_computation.9 | async-start | bytes 2228224 | tf_op jit(solution)/shard_map/all_gather | solution.py:110
  12.8 201.4 %all-gather.15.cloned.1.call-start = ((), (), s32[]{:S(2)}) async-start(), calls=%async_computation.12 | async-start | bytes 3145728 | tf_op jit(solution)/shard_map/all_gather | solution.py:144
  13.4 200.9 %all-gather.13.cloned.1.call-start = ((), (), s32[]{:S(2)}) async-start(), calls=%async_computation.10 | async-start | bytes 2228224 | tf_op jit(solution)/shard_map/all_gather | solution.py:114
  14.0 396.9 %all-reduce.26.cloned.1.call-start = ((), (), s32[]{:S(2)}) async-start(), calls=%async_computation.14 | async-start | bytes 1048576 | tf_op jit(solution)/shard_map/psum | solution.py:160
  14.7 47.8 %copy-start.64 = (f32[16]{0:T(128)}, f32[16]{0:T(128)S(1)}, u32[]{:S(2)}) copy-start(f32[16]{0:T(128)S(1)} %exponential_negate_fusion) | copy-start | bytes 196
  14.8 51.0 %copy-start.52 = (f32[1,256]{1,0:T(1,128)}, f32[1,256]{1,0:T(1,128)S(1)}, u32[]{:S(2)}) copy-start(f32[1,256]{1,0:T(1,128)S(1)} %get-tuple-element.395) | copy-start | bytes 3076
  14.8 51.0 %copy-start.54 = (f32[1,256]{1,0:T(1,128)}, f32[1,256]{1,0:T(1,128)S(1)}, u32[]{:S(2)}) copy-start(f32[1,256]{1,0:T(1,128)S(1)} %get-tuple-element.396) | copy-start | bytes 3076
  14.8 51.0 %copy-start.56 = (f32[1,256]{1,0:T(1,128)}, f32[1,256]{1,0:T(1,128)S(1)}, u32[]{:S(2)}) copy-start(f32[1,256]{1,0:T(1,128)S(1)} %get-tuple-element.397) | copy-start | bytes 3076
  14.8 51.0 %copy-start.58 = (f32[1,256]{1,0:T(1,128)}, f32[1,256]{1,0:T(1,128)S(1)}, u32[]{:S(2)}) copy-start(f32[1,256]{1,0:T(1,128)S(1)} %get-tuple-element.398) | copy-start | bytes 3076
  15.0 80.5 %copy-start.36 = (f32[1,1024]{1,0:T(1,128)}, f32[1,1024]{1,0:T(1,128)S(1)}, u32[]{:S(2)}) copy-start(f32[1,1024]{1,0:T(1,128)S(1)} %get-tuple-element.391) | copy-start | bytes 12292
  15.0 80.5 %copy-start.38 = (f32[1,1024]{1,0:T(1,128)}, f32[1,1024]{1,0:T(1,128)S(1)}, u32[]{:S(2)}) copy-start(f32[1,1024]{1,0:T(1,128)S(1)} %get-tuple-element.392) | copy-start | bytes 12292
  15.0 80.5 %copy-start.40 = (f32[1,1024]{1,0:T(1,128)}, f32[1,1024]{1,0:T(1,128)S(1)}, u32[]{:S(2)}) copy-start(f32[1,1024]{1,0:T(1,128)S(1)} %get-tuple-element.393) | copy-start | bytes 12292
  15.0 80.5 %copy-start.42 = (f32[1,1024]{1,0:T(1,128)}, f32[1,1024]{1,0:T(1,128)S(1)}, u32[]{:S(2)}) copy-start(f32[1,1024]{1,0:T(1,128)S(1)} %get-tuple-element.394) | copy-start | bytes 12292
  68.4 47.1 %copy-start.10 = (f32[1,1024,128]{2,1,0:T(8,128)}, f32[1,1024,128]{2,1,0:T(8,128)S(1)}, u32[]{:S(2)}) copy-start(f32[1,1024,128]{2,1,0:T(8,128)S(1)} %get-tuple-element.386) | copy-start | bytes 1572868
  68.5 91.7 %copy-start.30 = (f32[4,16,256]{2,1,0:T(8,128)}, f32[4,16,256]{2,1,0:T(8,128)S(1)}, u32[]{:S(2)}) copy-start(f32[4,16,256]{2,1,0:T(8,128)S(1)} %get-tuple-element.369) | copy-start | bytes 196612
  307.4 27.9 %copy-start.11 = (f32[1,1024,128]{2,1,0:T(8,128)S(1)}, f32[1,1024,128]{2,1,0:T(8,128)}, u32[]{:S(2)}) copy-start(f32[1,1024,128]{2,1,0:T(8,128)} %copy-done.10) | copy-start | bytes 1572868
  383.6 190.7 %reduce-scatter.22.cloned.1.call-start = ((), (), s32[]{:S(2)}) async-start(), calls=%async_computation.19 | async-start | bytes 278528
  390.0 185.6 %reduce-scatter.18.cloned.1.call-start = ((), (), s32[]{:S(2)}) async-start(), calls=%async_computation.17 | async-start | bytes 557056 | tf_op jit(solution)/shard_map/reduce_scatter | solution.py:205
  413.5 181.2 %reduce-scatter.20.cloned.1.call-start = ((), (), s32[]{:S(2)}) async-start(), calls=%async_computation.18 | async-start | bytes 2228224 | tf_op jit(solution)/shard_map/reduce_scatter | solution.py:214
  420.6 238.7 %reduce-scatter.14.cloned.1.call-start = ((), (), s32[]{:S(2)}) async-start(), calls=%async_computation.15 | async-start | bytes 2228224 | tf_op jit(solution)/shard_map/reduce_scatter | solution.py:193
  458.5 265.1 %reduce-scatter.16.cloned.1.call-start = ((), (), s32[]{:S(2)}) async-start(), calls=%async_computation.16 | async-start | bytes 2228224 | tf_op jit(solution)/shard_map/reduce_scatter | solution.py:199
  492.2 264.5 %reduce-scatter.12.cloned.1.call-start = ((), (), s32[]{:S(2)}) async-start(), calls=%async_computation.13 | async-start | bytes 3145728 | tf_op jit(solution)/shard_map/reduce_scatter | solution.py:180
  501.2 255.6 %copy-start.14 = (bf16[1,512,1024]{2,1,0:T(8,128)(2,1)S(1)}, bf16[1,512,1024]{2,1,0:T(8,128)(2,1)}, u32[]{:S(2)}) copy-start(bf16[1,512,1024]{2,1,0:T(8,128)(2,1)} %param.20) | copy-start | bytes 3145732
  501.2 255.6 %copy-start.27 = (bf16[1024,256]{1,0:T(8,128)(2,1)S(1)}, bf16[1024,256]{1,0:T(8,128)(2,1)}, u32[]{:S(2)}) copy-start(bf16[1024,256]{1,0:T(8,128)(2,1)} %copy-done.26) | copy-start | bytes 1572868
  501.2 255.5 %copy-start.46 = (f32[512]{0:T(512)S(1)}, f32[512]{0:T(512)}, u32[]{:S(2)}) copy-start(f32[512]{0:T(512)} %copy-done.45) | copy-start | bytes 6148
  501.2 255.5 %copy-start.49 = (f32[1024]{0:T(1024)S(1)}, f32[1024]{0:T(1024)}, u32[]{:S(2)}) copy-start(f32[1024]{0:T(1024)} %param.21) | copy-start | bytes 12292
  501.2 298.6 %reduce-scatter.10.cloned.1.call-start = ((), (), s32[]{:S(2)}) async-start(), calls=%async_computation.11 | async-start | bytes 3145728 | tf_op jit(solution)/shard_map/reduce_scatter | solution.py:140
  507.9 291.9 %copy-start.17 = (bf16[1,512,1024]{2,1,0:T(8,128)(2,1)S(1)}, bf16[1,512,1024]{2,1,0:T(8,128)(2,1)}, u32[]{:S(2)}) copy-start(bf16[1,512,1024]{2,1,0:T(8,128)(2,1)} %param.35) | copy-start | bytes 3145732
  (53 other events, 553.2 us)
Sparse Core Ops, SparseCore 0:
  11.5 35.8 all-gather.6
  49.5 41.3 all-gather.8
  93.1 40.1 all-gather.10
  134.7 31.8 all-gather.14
  168.6 41.3 all-gather.12
  383.7 27.1 all-reduce.25
  415.4 55.2 reduce-scatter.21
  475.2 54.8 reduce-scatter.17
  533.8 60.8 reduce-scatter.19
  598.7 60.5 reduce-scatter.13
  663.0 60.5 reduce-scatter.15
  725.8 30.8 reduce-scatter.11
  759.0 32.4 reduce-scatter.9
where the time goes:
time: 821 us; the launch traced here: 810 us
  waiting for transfers between devices  218 us (27%)
  matrix products  183 us (22%)
  blocking collectives  158 us (19%)
  local copies, waits for them, and re-layouts  127 us (15%)
  other arithmetic  109 us (13%)
  between operations  15.3 us (2%)
    reduce_scatter x1, waiting for transfers between devices, local(): lax.psum_scatter(weight_grad(gradient_gate_preactive).astype(jnp.bfloat16...  63 us
    reduce_scatter x1, waiting for transfers between devices, local(): lax.psum_scatter(weight_grad(gradient_input_preactive).astype(jnp.bfloat1...  62.7 us
    dot_general x3, matrix products, span_scan(): jnp.einsum('schqr,scrhp->scqhp', blended, sig_blk, precision=HIGH_ACCURACY)  61.9 us
    psum x1, blocking collectives, local(): lax.psum((pieces[4], conv_state_g, pieces[6], bias_state_g, pieces[8], pi...  61 us
    psum x1, blocking collectives, local(): norm_total = lax.psum(norm_part, ('dp', 'tensor'))  39.5 us
    reduce_scatter x1, waiting for transfers between devices, local(): lax.psum_scatter(back_terms.astype(jnp.bfloat16), 'tensor', scatter_dimen...  31.4 us
    dot_general x3, matrix products, span_scan(): jnp.einsum('scqn,schq,schnp->scqhp', c_blk, jnp.exp(cumulative), entering...  28.5 us
    all_gather x1, blocking collectives, local(): lax.all_gather(proj_step, 'dp', axis=0, tiled=True)  23.3 us
  transfers between devices with their start and end apart: 13, of which 6 were waited for; matrix products, arithmetic and copies ran while one was open for 30% of the time, Pallas kernels for 0%

commit v1 on v0

v1 whole, which is shorter than its diff:
```python
import jax
import jax.numpy as jnp
from jax import lax
from jax.experimental import pallas as pl
from jax.experimental.pallas import tpu as pltpu
from jax.sharding import PartitionSpec as P

SPAN = 256
DI = 2048
HEAD = 64
STATE = 128
EPS = 1e-05
F32 = jnp.float32
BF16 = jnp.bfloat16
VMEM_LIMIT = 48 * 1024 * 1024


def dot(a, b, ca, cb):
    return lax.dot_general(a, b, (((ca,), (cb,)), ((), ())), preferred_element_type=F32)


def sigmoid(v):
    return 1.0 / (1.0 + jnp.exp(-v))


def later(v, s):
    if s == 0:
        return v
    lane = lax.broadcasted_iota(jnp.int32, v.shape, 1)
    return jnp.where(lane >= s, pltpu.roll(v, s, 1), 0.0)


def earlier(v, s):
    if s == 0:
        return v
    length = v.shape[1]
    lane = lax.broadcasted_iota(jnp.int32, v.shape, 1)
    return jnp.where(lane < length - s, pltpu.roll(v, length - s, 1), 0.0)


def conv(x, par):
    v = par[:, 4:5] + par[:, 3:4] * x
    for k in range(3):
        v = v + par[:, k : k + 1] * later(x, 3 - k)
    return v


def conv_back(dv, par):
    g = par[:, 3:4] * dv
    for k in range(3):
        g = g + par[:, k : k + 1] * earlier(dv, 3 - k)
    return g


def total(v):
    return jnp.sum(v, axis=1, keepdims=True)


def columns(cols):
    lane = lax.broadcasted_iota(jnp.int32, (cols[0].shape[0], 128), 1)
    out = jnp.zeros(lane.shape, F32)
    for i, c in enumerate(cols):
        out = jnp.where(lane == i, c, out)
    return out


def decay(cq):
    q = cq.shape[1]
    col = jnp.broadcast_to(cq, (128, q)).T
    col = jnp.concatenate([col] * (q // 128), axis=1)
    r_pos = lax.broadcasted_iota(jnp.int32, (q, q), 0)
    q_pos = lax.broadcasted_iota(jnp.int32, (q, q), 1)
    return jnp.exp(jnp.where(q_pos >= r_pos, cq - col, -jnp.inf))


def fwd_kernel(xpre, gate, spre, rows, par, spar, y_out, mixed_out, sq_out, s_out, bc_out, scores):
    h = pl.program_id(0)
    blocks = scores.shape[0]

    @pl.when(h == 0)
    def _():
        v = conv(spre[...], spar[...])
        bc_out[...] = (v * sigmoid(v)).astype(BF16)
        sq_out[...] = jnp.zeros_like(sq_out)
        for c in range(blocks):
            sl = slice(c * SPAN, (c + 1) * SPAN)
            scores[c] = dot(bc_out[:STATE, sl], bc_out[STATE:, sl], 0, 0)

    v = conv(xpre[...], par[...])
    x = v * sigmoid(v)
    cum = rows[0:1, :]
    u = x * rows[1:2, :]
    ub = u.astype(BF16)
    state = jnp.zeros((HEAD, STATE), F32)
    for c in range(blocks):
        sl = slice(c * SPAN, (c + 1) * SPAN)
        cq = cum[:, sl]
        last = cq[:, SPAN - 1 :]
        pt = (scores[c] * decay(cq)).astype(BF16)
        sb = state.astype(BF16)
        s_out[c] = state
        y_out[:, sl] = dot(ub[:, sl], pt, 1, 0) + jnp.exp(cq) * dot(sb, bc_out[STATE:, sl], 1, 0)
        ute = (u[:, sl] * jnp.exp(last - cq)).astype(BF16)
        state = jnp.exp(last) * state + dot(ute, bc_out[:STATE, sl], 1, 1)
    g = gate[...]
    mixed = (y_out[...] + par[:, 5:6] * x) * (g * sigmoid(g))
    mixed_out[...] = mixed
    sq_out[...] += jnp.sum(mixed * mixed, axis=0, keepdims=True)


def bwd_kernel(
    xpre, gate, y_in, gg_in, s_in, rows, tok, bc, par,
    gx_out, ggate_out, cols_out, rows_out, dbc_out, scores, dscores, dbc,
):
    h = pl.program_id(0)
    blocks = scores.shape[0]

    @pl.when(h == 0)
    def _():
        for c in range(blocks):
            sl = slice(c * SPAN, (c + 1) * SPAN)
            scores[c] = dot(bc[:STATE, sl], bc[STATE:, sl], 0, 0)
        dscores[...] = jnp.zeros_like(dscores)
        dbc[...] = jnp.zeros_like(dbc)

    x0 = xpre[...]
    v = conv(x0, par[...])
    sg = sigmoid(v)
    x = v * sg
    skip = par[:, 5:6]
    cum = rows[0:1, :]
    dt = rows[1:2, :]
    scale = tok[0:1, :]
    g = gate[...]
    sgate = sigmoid(g)
    silu_g = g * sgate
    y = y_in[...]
    gg = gg_in[...]
    scanned = y + skip * x
    mixed = scanned * silu_g
    gm = scale * gg * par[:, 6:7] - mixed * tok[1:2, :]
    ggate_out[...] = (gm * scanned * (sgate * (1.0 + g * (1.0 - sgate)))).astype(BF16)
    dgain = total(gg * mixed * scale)
    dy = gm * silu_g
    dskip = total(dy * x)
    dyb = dy.astype(BF16)
    dyf = dyb.astype(F32)
    out_dot = jnp.sum(dyf * y, axis=0, keepdims=True)
    u = x * dt
    ub = u.astype(BF16)
    uf = ub.astype(F32)
    lane = lax.broadcasted_iota(jnp.int32, (1, SPAN), 1)
    grad = jnp.zeros((HEAD, STATE), F32)
    du_parts = []
    dcum_parts = []
    for c in reversed(range(blocks)):
        sl = slice(c * SPAN, (c + 1) * SPAN)
        cq = cum[:, sl]
        last = cq[:, SPAN - 1 :]
        te = jnp.exp(last - cq)
        ec = jnp.exp(cq)
        b_c = bc[:STATE, sl]
        c_c = bc[STATE:, sl]
        w = decay(cq)
        pt = (scores[c] * w).astype(BF16)
        dpt = dot(ub[:, sl], dyb[:, sl], 0, 0)
        dscores[c] += dpt * w
        gb = grad.astype(BF16)
        state = s_in[c]
        du1 = dot(dyb[:, sl], pt, 1, 1)
        du2 = dot(gb, b_c, 1, 0) * te
        du = du1 + du2
        through = uf[:, sl] * du2
        at_end = jnp.sum(through) + jnp.sum(jnp.exp(last) * grad * state)
        dc = out_dot[:, sl] - jnp.sum(uf[:, sl] * du1 + through, axis=0, keepdims=True)
        dcum_parts.append(dc + jnp.where(lane == SPAN - 1, at_end, 0.0))
        du_parts.append(du)
        edy = (dyf[:, sl] * ec).astype(BF16)
        dbc[STATE:, sl] += dot(state.astype(BF16), edy, 0, 0)
        dbc[:STATE, sl] += dot(gb, (u[:, sl] * te).astype(BF16), 0, 0)
        grad = jnp.exp(last) * grad + dot(edy, c_c, 1, 1)
    du = jnp.concatenate(du_parts[::-1], axis=1)
    rows_out[0:1, :] = jnp.concatenate(dcum_parts[::-1], axis=1)
    rows_out[1:2, :] = jnp.sum(x * du, axis=0, keepdims=True)
    dv = (du * dt + skip * dy) * (sg * (1.0 + v * (1.0 - sg)))
    gx_out[...] = conv_back(dv, par[...]).astype(BF16)
    cols = [total(dv * later(x0, 3 - k)) for k in range(4)]
    cols_out[...] = columns(cols + [total(dv), dskip, dgain])

    @pl.when(h == pl.num_programs(0) - 1)
    def _():
        for c in range(blocks):
            sl = slice(c * SPAN, (c + 1) * SPAN)
            ds = dscores[c].astype(BF16)
            dbc_out[:STATE, sl] = (dbc[:STATE, sl] + dot(bc[STATE:, sl], ds, 1, 1)).astype(BF16)
            dbc_out[STATE:, sl] = (dbc[STATE:, sl] + dot(bc[:STATE, sl], ds, 1, 0)).astype(BF16)


def state_kernel(spre, dbc, spar, g_out, cols_out):
    x0 = spre[...]
    v = conv(x0, spar[...])
    sg = sigmoid(v)
    dv = dbc[...].astype(F32) * (sg * (1.0 + v * (1.0 - sg)))
    g_out[...] = conv_back(dv, spar[...]).astype(BF16)
    cols = [total(dv * later(x0, 3 - k)) for k in range(4)]
    cols_out[...] = columns(cols + [total(dv)])


def cost(flops, size):
    return pl.CostEstimate(flops=flops, bytes_accessed=size, transcendentals=0)


PARAMS = pltpu.CompilerParams(
    dimension_semantics=("arbitrary",), vmem_limit_bytes=VMEM_LIMIT
)


def specs(length):
    chan = pl.BlockSpec((HEAD, length), lambda h: (h, 0))
    rows = pl.BlockSpec((None, 2, length), lambda h: (h, 0, 0))
    par = pl.BlockSpec((HEAD, 8), lambda h: (h, 0))
    states = pl.BlockSpec((None, length // SPAN, HEAD, STATE), lambda h: (h, 0, 0, 0))
    whole = lambda *shape: pl.BlockSpec(shape, lambda h: (0,) * len(shape))
    return chan, rows, par, states, whole


def scan_fwd(xpre, gate, spre, rows, par, spar):
    inner, length = xpre.shape
    heads, blocks = inner // HEAD, length // SPAN
    chan, row, parb, states, whole = specs(length)
    sds = jax.ShapeDtypeStruct
    return pl.pallas_call(
        fwd_kernel,
        grid=(heads,),
        in_specs=[chan, chan, whole(2 * STATE, length), row, parb, whole(2 * STATE, 8)],
        out_specs=[chan, chan, whole(1, length), states, whole(2 * STATE, length)],
        out_shape=[
            sds((inner, length), F32),
            sds((inner, length), F32),
            sds((1, length), F32),
            sds((heads, blocks, HEAD, STATE), F32),
            sds((2 * STATE, length), BF16),
        ],
        scratch_shapes=[pltpu.VMEM((blocks, SPAN, SPAN), F32)],
        compiler_params=PARAMS,
        cost_estimate=cost(12 * 10**9, 20 * 10**6),
    )(xpre, gate, spre, rows, par, spar)


def scan_bwd(xpre, gate, y, gg, states_in, rows, tok, bc, par):
    inner, length = xpre.shape
    heads, blocks = inner // HEAD, length // SPAN
    chan, row, parb, states, whole = specs(length)
    sds = jax.ShapeDtypeStruct
    return pl.pallas_call(
        bwd_kernel,
        grid=(heads,),
        in_specs=[
            chan, chan, chan, chan, states, row,
            whole(2, length), whole(2 * STATE, length), parb,
        ],
        out_specs=[
            chan, chan, pl.BlockSpec((HEAD, 128), lambda h: (h, 0)), row,
            whole(2 * STATE, length),
        ],
        out_shape=[
            sds((inner, length), BF16),
            sds((inner, length), BF16),
            sds((inner, 128), F32),
            sds((heads, 2, length), F32),
            sds((2 * STATE, length), BF16),
        ],
        scratch_shapes=[
            pltpu.VMEM((blocks, SPAN, SPAN), F32),
            pltpu.VMEM((blocks, SPAN, SPAN), F32),
            pltpu.VMEM((2 * STATE, length), F32),
        ],
        compiler_params=PARAMS,
        cost_estimate=cost(30 * 10**9, 30 * 10**6),
    )(xpre, gate, y, gg, states_in, rows, tok, bc, par)


def state_bwd(spre, dbc, spar):
    sds = jax.ShapeDtypeStruct
    return pl.pallas_call(
        state_kernel,
        out_shape=[sds(spre.shape, BF16), sds((spre.shape[0], 128), F32)],
        compiler_params=pltpu.CompilerParams(vmem_limit_bytes=VMEM_LIMIT),
        cost_estimate=cost(10**9, 2 * 10**6),
    )(spre, dbc, spar)


def bits_of(n):
    return n.bit_length() - 1


def swap(v, axis, n, bit):
    return lax.ppermute(v, axis, [(i, i ^ (1 << bit)) for i in range(n)])


def sum_all(v, axis, n):
    for bit in range(bits_of(n)):
        v = v + swap(v, axis, n, bit)
    return v


def sum_scatter(v, axis, n, order, last=F32):
    me = lax.axis_index(axis)
    rows, rest = v.shape[0] // n, v.shape[1:]
    left = list(range(bits_of(n)))[::-1]
    v = v.reshape((2,) * len(left) + (rows,) + rest)
    for i, bit in enumerate(order):
        dim = left.index(bit)
        mine = (me >> bit) & 1
        keep = lax.dynamic_index_in_dim(v, mine, dim, keepdims=False)
        send = lax.dynamic_index_in_dim(v, 1 - mine, dim, keepdims=False)
        left.remove(bit)
        got = swap(send, axis, n, bit)
        v = keep.astype(F32) + got.astype(F32)
        if i < len(order) - 1:
            v = v.astype(BF16)
    return v.astype(last)


def local(
    dp_size,
    tp_size,
    stream,
    norm_gain,
    proj_gate,
    proj_input,
    proj_state,
    proj_step,
    conv_input,
    conv_state,
    bias_input,
    bias_state,
    step_bias,
    decay_log,
    skip_gain,
    gate_gain,
    proj_output,
    cotangent,
):
    inner = conv_input.shape[1]
    heads = inner // HEAD
    own_rows = stream.shape[1]
    length = own_rows * tp_size
    blocks = length // SPAN
    dp_order = [0, 1] + list(range(bits_of(dp_size)))[2:][::-1]
    tp_order = list(range(bits_of(tp_size)))[::-1]
    stream_f = stream[0].astype(F32)
    inv_rms = lax.rsqrt(jnp.mean(stream_f * stream_f, axis=-1, keepdims=True) + EPS)
    normed = stream_f * inv_rms
    own_hidden = (normed * norm_gain).astype(BF16)
    hidden = lax.all_gather(own_hidden, "tensor", axis=0, tiled=True)
    cot = lax.all_gather(cotangent[0], "tensor", axis=0, tiled=True)
    input_w = lax.all_gather(proj_input, "dp", axis=0, tiled=True)
    small_w = lax.all_gather(
        jnp.concatenate([proj_state, proj_step], axis=1), "dp", axis=0, tiled=True
    )
    gate_w = lax.all_gather(proj_gate, "dp", axis=0, tiled=True)
    out_w = lax.all_gather(proj_output.T, "dp", axis=0, tiled=True)
    n_state = proj_state.shape[1]

    def project(w):
        return jnp.einsum("lp,pr->rl", hidden, w, preferred_element_type=F32)

    input_pre = project(input_w)
    small_pre = project(small_w)
    state_pre, step_pre = small_pre[:n_state], small_pre[n_state:]
    gate_pre = project(gate_w)

    step_in = step_pre + step_bias[:, None]
    dt = jax.nn.softplus(step_in)
    neg = -jnp.exp(decay_log)[:, None]
    rate = neg * dt
    tri = jnp.triu(jnp.ones((SPAN, SPAN), F32))
    cum = jnp.einsum(
        "hbt,tq->hbq", rate.reshape(heads, blocks, SPAN), tri, precision=lax.Precision.HIGHEST
    ).reshape(heads, length)
    rows = jnp.stack([cum, dt], axis=1)
    zero = jnp.zeros((inner, 1), F32)
    par = jnp.concatenate(
        [
            conv_input.T,
            bias_input[:, None],
            jnp.repeat(skip_gain, HEAD)[:, None],
            gate_gain[:, None],
            zero,
        ],
        axis=1,
    )
    spar = jnp.concatenate(
        [conv_state.T, bias_state[:, None], jnp.zeros((n_state, 3), F32)], axis=1
    )
    y, mixed, square, states, bc = scan_fwd(input_pre, gate_pre, state_pre, rows, par, spar)

    grad_gated = jnp.einsum("le,ec->cl", cot, out_w, preferred_element_type=F32)
    inner_dot = jnp.sum(grad_gated * gate_gain[:, None] * mixed, axis=0, keepdims=True)
    sums = sum_all(jnp.concatenate([square, inner_dot], axis=0), "tensor", tp_size)
    scale = lax.rsqrt(sums[0:1] / DI + EPS)
    tok = jnp.concatenate([scale, scale * scale * scale * (sums[1:2] / DI)], axis=0)
    gated = (mixed * scale * gate_gain[:, None]).astype(BF16)
    grad_out_w = jnp.einsum("cl,le->ec", gated, cot, preferred_element_type=F32).astype(BF16)
    shard_out = sum_scatter(grad_out_w, "dp", dp_size, dp_order)
    partial_out = jnp.einsum("cl,ec->le", gated, out_w, preferred_element_type=F32).astype(BF16)
    branch = sum_scatter(partial_out, "tensor", tp_size, tp_order)
    output = (stream_f + branch).astype(BF16)

    gx, ggate, cols, drows, dbc = scan_bwd(
        input_pre, gate_pre, y, grad_gated, states, rows, tok, bc, par
    )
    dbc_total = sum_all(dbc.astype(BF16), "tensor", tp_size)
    gstate, scols = state_bwd(state_pre, dbc_total, spar)
    drate = jnp.einsum(
        "hbt,qt->hbq",
        drows[:, 0].reshape(heads, blocks, SPAN),
        tri,
        precision=lax.Precision.HIGHEST,
    ).reshape(heads, length)
    ddt = drows[:, 1] + drate * neg
    ddecay = jnp.sum(drate * rate, axis=1)
    dstep = ddt * jax.nn.sigmoid(step_in)
    dstep_bias = jnp.sum(dstep, axis=1)
    gstep = dstep.astype(BF16)

    def weight_grad(g):
        return jnp.einsum("lk,cl->kc", hidden, g, preferred_element_type=F32).astype(BF16)

    shard_input = sum_scatter(weight_grad(gx), "dp", dp_size, dp_order)
    shard_gate = sum_scatter(weight_grad(ggate), "dp", dp_size, dp_order)
    shard_small = sum_scatter(
        weight_grad(jnp.concatenate([gstate, gstep], axis=0)), "dp", dp_size, dp_order
    )

    def back(g, w):
        return jnp.einsum("cl,nc->ln", g, w, preferred_element_type=F32)

    state_w, step_w = small_w[:, :n_state], small_w[:, n_state:]
    back_terms = back(ggate, gate_w) + back(gx, input_w) + back(gstep, step_w)
    grad_hidden = sum_scatter(back_terms.astype(BF16), "tensor", tp_size, tp_order)
    row_start = lax.axis_index("tensor") * own_rows
    own_gstate = lax.dynamic_slice_in_dim(gstate, row_start, own_rows, 1)
    grad_hidden = grad_hidden + back(own_gstate, state_w)
    weighted_h = grad_hidden * norm_gain
    norm_dot = jnp.mean(weighted_h * normed, axis=-1, keepdims=True)
    grad_stream = (
        cotangent[0].astype(F32) + inv_rms * (weighted_h - normed * norm_dot)
    ).astype(BF16)
    norm_part = sum_all(jnp.sum(grad_hidden * normed, axis=0), "tensor", tp_size)

    pieces = [
        cols[:, :4].T,
        cols[:, 4],
        jnp.sum(cols[:, 5].reshape(heads, HEAD), axis=1),
        cols[:, 6],
        scols[:, :4].T,
        scols[:, 4],
        dstep_bias,
        ddecay,
        norm_part,
    ]
    flat = jnp.concatenate([p.reshape(-1) for p in pieces])
    pad = -flat.shape[0] % 1024
    flat = jnp.pad(flat, (0, pad)).reshape(-1, 128)
    flat = sum_all(flat, "dp", dp_size).reshape(-1)
    done, at = [], 0
    for p in pieces:
        done.append(flat[at : at + p.size].reshape(p.shape))
        at += p.size
    conv_in_g, bias_in_g, skip_g, gain_g, conv_st_g, bias_st_g, step_b_g, decay_g, norm_g = done
    return (
        output[None],
        grad_stream[None],
        norm_g,
        shard_gate,
        shard_input,
        shard_small[:, :n_state],
        shard_small[:, n_state:],
        conv_in_g,
        conv_st_g,
        bias_in_g,
        bias_st_g,
        step_b_g,
        decay_g,
        skip_g,
        gain_g,
        shard_out.T,
    )


def solution(mesh):
    placed = (
        P("dp", "tensor", None),
        P(),
        P("dp", "tensor"),
        P("dp", "tensor"),
        P("dp", None),
        P("dp", "tensor"),
        P(None, "tensor"),
        P(),
        P("tensor"),
        P(),
        P("tensor"),
        P("tensor"),
        P("tensor"),
        P("tensor"),
        P("tensor", "dp"),
        P("dp", "tensor", None),
    )
    dp_size, tp_size = mesh.shape["dp"], mesh.shape["tensor"]

    def run(*args):
        return local(dp_size, tp_size, *args)

    return jax.shard_map(
        run,
        mesh=mesh,
        in_specs=placed,
        out_specs=(
            P("dp", "tensor", None),
            P("dp", "tensor", None),
            P(),
            P("dp", "tensor"),
            P("dp", "tensor"),
            P("dp", None),
            P("dp", "tensor"),
            P(None, "tensor"),
            P(),
            P("tensor"),
            P(),
            P("tensor"),
            P("tensor"),
            P("tensor"),
            P("tensor"),
            P("tensor", "dp"),
        ),
        check_vma=False,
    )
```

time: 821 us -> 430 us (0.52)
  blocking collectives: 158 us -> 25.5 us
  matrix products: 183 us -> 52.7 us
  local copies, waits for them, and re-layouts: 127 us -> 26 us
  other arithmetic: 109 us -> 21.6 us
  Pallas kernels: 0 us -> 67.8 us
  waiting for transfers between devices: 218 us -> 196 us
  starting transfers between devices: 1.31 us -> 18.6 us
    reduce_scatter x6 -> x0, waiting for transfers between devices: 175 us -> none  [the longest x1 63 us: local(): lax.psum_scatter(weight_grad(gradient_gate_preactive).astype(jnp.bfloat16...]
    dot_general x27 -> x15, matrix products: 183 us -> 52.7 us  [the longest x4 17.1 us: back(): return jnp.einsum('cl,nc->ln', g, w, preferred_element_type=F32)]
    psum x5 -> x0, blocking collectives: 115 us -> none  [the longest x1 61 us: local(): lax.psum((pieces[4], conv_state_g, pieces[6], bias_state_g, pieces[8], pi...]
    all_gather x5, waiting for transfers between devices: 19.8 us -> 130 us  [the longest x1 43.4 us: local(): out_w = lax.all_gather(proj_output.T, 'dp', axis=0, tiled=True)]
    pallas_call x0 -> x3, Pallas kernels: none -> 67.8 us  [the longest x1 44.6 us: scan_bwd(): pl.pallas_call(bwd_kernel, grid=(heads,), in_specs=[chan, chan, chan, cha...]
    ppermute x0 -> x25, waiting for transfers between devices: none -> 63.2 us  [swap(): return lax.ppermute(v, axis, [(i, i ^ 1 << bit) for i in range(n)])]
    reshape x12 -> x4, local copies, waits for them, and re-layouts: 55.9 us -> 1.23 us  [the longest x2 1.21 us: local(): done.append(flat[at:at + p.size].reshape(p.shape))]
    reduce_sum x11 -> x2, other arithmetic: 34.7 us -> 1.16 us  [the longest x1 1.04 us: local(): dstep_bias = jnp.sum(dstep, axis=1)]
  transfers between devices with their start and end apart: 13 -> 30, of which waited for: 6 -> 19; matrix products, arithmetic and copies ran while one was open for 30% -> 19% of each run, Pallas kernels for 0% -> 5%
where the time goes in v1:
time: 430 us; the launch traced here: 423 us
  waiting for transfers between devices  196 us (46%)
  Pallas kernels  67.8 us (16%)
  matrix products  52.7 us (12%)
  local copies, waits for them, and re-layouts  26 us (6%)
  blocking collectives  25.5 us (6%)
  other arithmetic  21.6 us (5%)
  starting transfers between devices  18.6 us (4%)
  between operations  14.8 us (3%)
    ppermute x25, waiting for transfers between devices, swap(): return lax.ppermute(v, axis, [(i, i ^ 1 << bit) for i in range(n)])  63.2 us
    pallas_call x1, Pallas kernels, scan_bwd(): pl.pallas_call(bwd_kernel, grid=(heads,), in_specs=[chan, chan, chan, cha...  44.6 us
    all_gather x1, waiting for transfers between devices, local(): out_w = lax.all_gather(proj_output.T, 'dp', axis=0, tiled=True)  43.4 us
    all_gather x1, waiting for transfers between devices, local(): gate_w = lax.all_gather(proj_gate, 'dp', axis=0, tiled=True)  39.2 us
    all_gather x1, waiting for transfers between devices, local(): input_w = lax.all_gather(proj_input, 'dp', axis=0, tiled=True)  35.7 us
    all_gather x1, blocking collectives, local(): lax.all_gather(jnp.concatenate([proj_state, proj_step], axis=1), 'dp', ax...  25.5 us
    pallas_call x1, Pallas kernels, scan_fwd(): pl.pallas_call(fwd_kernel, grid=(heads,), in_specs=[chan, chan, whole(2 *...  20.3 us
    ppermute x25, starting transfers between devices, swap(): return lax.ppermute(v, axis, [(i, i ^ 1 << bit) for i in range(n)])  18.4 us
  transfers between devices with their start and end apart: 30, of which 19 were waited for; matrix products, arithmetic and copies ran while one was open for 19% of the time, Pallas kernels for 5%

profile of v1, /device:TPU:0, one launch (start us, length us, event | category | flops | bytes accessed | tf_op | source)
XLA Modules:
  0.0 423.2 jit_solution(18143984870201175595)
XLA Ops:
  8.8 2.5 fusion.4
  14.9 25.5 %all_gather.21 = bf16[1024,272]{1,0:T(8,128)(2,1)S(1)} all-gather(bf16[64,272]{1,0:T(8,128)(2,1)S(1)} %pad_maximum_fusion.1), channel_id=1, replica_groups=mesh['dp'=16,'tensor'=2] {'dp'}, dimensions={0}, use_global_device_ids=true | all-gather | bytes 591872 | tf_op jit(solution)/shard_map/all_gather | solution.py:359
  40.4 6.9 %all-gather.7.cloned.1.call-done = bf16[1024,1024]{1,0:T(8,128)(2,1)} async-done(((bf16[512,1024]{1,0:T(8,128)(2,1)}), bf16[1024,1024]{1,0:T(8,128)(2,1)}) %all-gather.7.cloned.1.call-update) | async-done | bytes 2097168 | tf_op jit(solution)/shard_map/all_gather | solution.py:356
  47.4 2.6 fusion.79
  51.8 39.2 %all-gather.11.cloned.1.call-done = bf16[1024,1024]{1,0:T(8,128)(2,1)} async-done(((bf16[64,1024]{1,0:T(8,128)(2,1)}), bf16[1024,1024]{1,0:T(8,128)(2,1)}) %all-gather.11.cloned.1.call-update) | async-done | bytes 2097168 | tf_op jit(solution)/shard_map/all_gather | solution.py:362
  91.0 6.7 %convolution_bitcast_fusion.gate = f32[1024,1024]{1,0:T(8,128)} fusion(bf16[1024,1024]{1,0:T(8,128)(2,1)} %all-gather.7.cloned.1.call-done, bf16[1024,1024]{1,0:T(8,128)(2,1)} %all-gather.11.cloned.1.call-done), kind=kOutput, calls=%fused_computation.10 | convolution fusion | flops 2147483648 | bytes 8388608 | tf_op jit(solution)/shard_map/lp,pr->rl/dot_general | solution.py:367
  97.6 35.7 %all-gather.9.cloned.1.call-done = bf16[1024,1024]{1,0:T(8,128)(2,1)} async-done(((bf16[64,1024]{1,0:T(8,128)(2,1)}), bf16[1024,1024]{1,0:T(8,128)(2,1)}) %all-gather.9.cloned.1.call-update) | async-done | bytes 2097168 | tf_op jit(solution)/shard_map/all_gather | solution.py:358
  133.3 6.6 %convolution_bitcast_fusion.1.xpre = f32[1024,1024]{1,0:T(8,128)} fusion(bf16[1024,1024]{1,0:T(8,128)(2,1)} %all-gather.7.cloned.1.call-done, bf16[1024,1024]{1,0:T(8,128)(2,1)} %all-gather.9.cloned.1.call-done), kind=kOutput, calls=%fused_computation.11 | convolution fusion | flops 2147483648 | bytes 8388608 | tf_op jit(solution)/shard_map/lp,pr->rl/dot_general | solution.py:367
  140.0 20.3 %shard_map.279 = (f32[1024,1024]{1,0:T(8,128)}, f32[1024,1024]{1,0:T(8,128)}, f32[1,1024]{1,0:T(1,128)S(1)}, f32[16,4,64,128]{3,2,1,0:T(8,128)S(1)}, bf16[256,1024]{1,0:T(8,128)(2,1)S(1)}) custom-call(f32[1024,1024]{1,0:T(8,128)} %convolution_bitcast_fusion.1.xpre, f32[1024,1024]{1,0:T(8,128)} %convolution_bitcast_fusion.gate, f32[256,1024]{1,0:T(8,128)S(1)} %slice.105.spre, ...), custom_call_target="tpu_custom_call" | custom-call | flops 12000000000 | bytes 20000000 | tf_op jit(solution)/shard_map/pallas_call | solution.py:232
  161.6 5.1 %all-gather.15.cloned.1.call-done = bf16[1,1024,1024]{2,1,0:T(8,128)(2,1)} async-done(((bf16[1,512,1024]{2,1,0:T(8,128)(2,1)}), bf16[1,1024,1024]{2,1,0:T(8,128)(2,1)}) %all-gather.15.cloned.1.call-update) | async-done | bytes 2097168 | tf_op jit(solution)/shard_map/all_gather | solution.py:357
  166.6 43.4 %all-gather.13.cloned.1.call-done = bf16[1024,1024]{1,0:T(8,128)(2,1)} async-done(((bf16[64,1024]{1,0:T(8,128)(2,1)}), bf16[1024,1024]{1,0:T(8,128)(2,1)}) %all-gather.13.cloned.1.call-update) | async-done | bytes 2097168 | tf_op jit(solution)/shard_map/all_gather | solution.py:363
  210.1 8.0 %multiply_reduce_fusion = (f32[1024]{0:T(1024)S(1)}, f32[1024,1024]{1,0:T(8,128)}) fusion(f32[1024,1024]{1,0:T(8,128)} %get-tuple-element.28, f32[1024]{0:T(1024)S(1)} %copy-done.23, bf16[1024,1024]{1,0:T(8,128)(2,1)} %all-gather.13.cloned.1.call-done, bf16[1,1024,1024]{2,1,0:T(8,128)(2,1)} %all-gather.15.cloned.1.call-done), kind=kOutput, calls=%fused_computation.2 | convolution fusion | flops 2150628352 | bytes 12591104 | tf_op jit(solution)/shard_map/le,ec->cl/dot_general | solution.py:399
  222.0 44.6 %shard_map.280 = (bf16[1024,1024]{1,0:T(8,128)(2,1)S(1)}, bf16[1024,1024]{1,0:T(8,128)(2,1)}, f32[1024,128]{1,0:T(8,128)S(1)}, f32[16,2,1024]{2,1,0:T(2,128)S(1)}, bf16[256,1024]{1,0:T(8,128)(2,1)S(1)}) custom-call(f32[1024,1024]{1,0:T(8,128)} %convolution_bitcast_fusion.1.xpre, f32[1024,1024]{1,0:T(8,128)} %convolution_bitcast_fusion.gate, ...), custom_call_target="tpu_custom_call" | custom-call | flops 30000001024 | bytes 30000000 | tf_op jit(solution)/shard_map/pallas_call | solution.py:255
  268.8 2.6 convolution_convert_fusion.2
  274.1 2.4 convolution_convert_fusion.1
  278.5 2.7 fusion.21
  281.2 2.4 convolution_convert_fusion
  290.4 4.6 %fusion.80 = f32[1024,1024]{1,0:T(8,128)} fusion(bf16[1024,1024]{1,0:T(8,128)(2,1)S(1)} %copy-done.35, bf16[1024,1024]{1,0:T(8,128)(2,1)S(1)} %copy-done.28), kind=kOutput, calls=%fused_computation.160 | convolution fusion | flops 2147483648 | bytes 8388608 | tf_op jit(solution)/shard_map/cl,nc->ln/dot_general | solution.py:438
  295.0 4.4 %fusion.81 = f32[1024,1024]{1,0:T(8,128)} fusion(bf16[1024,1024]{1,0:T(8,128)(2,1)S(1)} %get-tuple-element.34, bf16[1024,1024]{1,0:T(8,128)(2,1)S(1)} %copy-done.29), kind=kOutput, calls=%fused_computation.161 | convolution fusion | flops 2147483648 | bytes 8388608 | tf_op jit(solution)/shard_map/cl,nc->ln/dot_general | solution.py:438
  299.6 3.0 shard_map.281
  306.4 4.3 %add_convert_fusion = bf16[1024,1024]{1,0:T(8,128)(2,1)S(1)} fusion(f32[1024,1024]{1,0:T(8,128)} %fusion.80, f32[1024,1024]{1,0:T(8,128)} %fusion.81, bf16[16,1024]{1,0:T(8,128)(2,1)S(1)} %get-tuple-element.94, bf16[1024,272]{1,0:T(8,128)(2,1)} %copy-done.14), kind=kOutput, calls=%fused_computation | convolution fusion | flops 36700160 | bytes 10780672 | tf_op jit(solution)/shard_map/cl,nc->ln/dot_general | solution.py:438
  314.5 6.6 %collective-permute-done.19 = bf16[2,64,272]{2,1,0:T(8,128)(2,1)S(1)} collective-permute-done((bf16[2,64,272]{2,1,0:T(8,128)(2,1)S(1)}, bf16[2,64,272]{2,1,0:T(8,128)(2,1)S(1)}, u32[]{:S(2)}, u32[]{:S(2)}) %collective-permute-start.19) | collective-permute-done | bytes 69664 | tf_op jit(solution)/shard_map/ppermute | solution.py:298
  321.4 3.8 collective-permute-done.20
  331.6 6.6 %collective-permute-done.2 = bf16[512,1024]{1,0:T(8,128)(2,1)} collective-permute-done((bf16[512,1024]{1,0:T(8,128)(2,1)}, bf16[512,1024]{1,0:T(8,128)(2,1)}, u32[]{:S(2)}, u32[]{:S(2)}) %collective-permute-start.2) | collective-permute-done | bytes 1048608 | tf_op jit(solution)/shard_map/ppermute | solution.py:298
  338.3 3.8 fusion.10
  351.7 9.4 %collective-permute-done.6 = f32[72,128]{1,0:T(8,128)S(1)} collective-permute-done((f32[72,128]{1,0:T(8,128)S(1)}, f32[72,128]{1,0:T(8,128)S(1)}, u32[]{:S(2)}, u32[]{:S(2)}) %collective-permute-start.6) | collective-permute-done | bytes 36896 | tf_op jit(solution)/shard_map/ppermute | solution.py:298
  361.7 3.4 collective-permute-done.7
  365.8 4.3 %fusion.25 = (bf16[1,512,1024]{2,1,0:T(8,128)(2,1)}, bf16[1,512,1024]{2,1,0:T(8,128)(2,1)}) fusion(f32[512,1024]{1,0:T(8,128)} %get-tuple-element.116, bf16[1,512,1024]{2,1,0:T(8,128)(2,1)S(1)} %copy-done.7, bf16[1,512,1024]{2,1,0:T(8,128)(2,1)S(1)} %copy-done.1, f32[512]{0:T(512)S(1)} %broadcast_multiply_fusion.1, f32[1024]{0:T(1024)S(1)} %copy-done.18, ...), kind=kLoop, calls=%fused_computation.41 | loop fusion | flops 7340032 | bytes 8396804 | tf_op jit(solution)/shard_map/broadcast_in_dim | solution.py:475
  383.1 14.2 %collective-permute-done.11 = bf16[2,64,1024]{2,1,0:T(8,128)(2,1)S(1)} collective-permute-done((bf16[2,64,1024]{2,1,0:T(8,128)(2,1)S(1)}, bf16[2,64,1024]{2,1,0:T(8,128)(2,1)S(1)}, u32[]{:S(2)}, u32[]{:S(2)}) %collective-permute-start.11) | collective-permute-done | bytes 262176 | tf_op jit(solution)/shard_map/ppermute | solution.py:298
  397.5 5.5 %collective-permute-done.15 = bf16[2,64,1024]{2,1,0:T(8,128)(2,1)S(1)} collective-permute-done((bf16[2,64,1024]{2,1,0:T(8,128)(2,1)S(1)}, bf16[2,64,1024]{2,1,0:T(8,128)(2,1)S(1)}, u32[]{:S(2)}, u32[]{:S(2)}) %collective-permute-start.15) | collective-permute-done | bytes 262176 | tf_op jit(solution)/shard_map/ppermute | solution.py:298
  403.2 4.1 collective-permute-done.23
  407.5 2.6 collective-permute-done.12
  (221 shorter events, 70.3 us)
Async XLA Ops:
  7.2 40.2 %all-gather.7.cloned.1.call-start = ((), (), s32[]{:S(2)}) async-start(), calls=%async_computation | async-start | bytes 3145728 | tf_op jit(solution)/shard_map/all_gather | solution.py:356
  11.4 79.6 %all-gather.11.cloned.1.call-start = ((), (), s32[]{:S(2)}) async-start(), calls=%async_computation.2 | async-start | bytes 2228224 | tf_op jit(solution)/shard_map/all_gather | solution.py:362
  12.1 121.2 %all-gather.9.cloned.1.call-start = ((), (), s32[]{:S(2)}) async-start(), calls=%async_computation.1 | async-start | bytes 2228224 | tf_op jit(solution)/shard_map/all_gather | solution.py:358
  12.9 153.8 %all-gather.15.cloned.1.call-start = ((), (), s32[]{:S(2)}) async-start(), calls=%async_computation.4 | async-start | bytes 3145728 | tf_op jit(solution)/shard_map/all_gather | solution.py:357
  13.5 196.6 %all-gather.13.cloned.1.call-start = ((), (), s32[]{:S(2)}) async-start(), calls=%async_computation.3 | async-start | bytes 2228224 | tf_op jit(solution)/shard_map/all_gather | solution.py:363
  218.2 3.7 collective-permute-start
  221.9 46.8 %copy-start.31 = (bf16[1024,1024]{1,0:T(8,128)(2,1)S(1)}, bf16[1024,1024]{1,0:T(8,128)(2,1)}, u32[]{:S(2)}) copy-start(bf16[1024,1024]{1,0:T(8,128)(2,1)} %all-gather.13.cloned.1.call-done) | copy-start | bytes 6291460
  221.9 46.8 %copy-start.33 = (f32[1024,1024]{1,0:T(8,128)S(1)}, f32[1024,1024]{1,0:T(8,128)}, u32[]{:S(2)}) copy-start(f32[1024,1024]{1,0:T(8,128)} %get-tuple-element.28) | copy-start | bytes 12582916
  267.2 32.2 %collective-permute-start.3 = (bf16[256,1024]{1,0:T(8,128)(2,1)S(1)}, bf16[256,1024]{1,0:T(8,128)(2,1)S(1)}, u32[]{:S(2)}, u32[]{:S(2)}) collective-permute-start(bf16[256,1024]{1,0:T(8,128)(2,1)S(1)} %get-tuple-element.36), channel_id=1, source_target_pairs={{0,1},{1,0},{2,3},{3,2},{4,5},{5,4},{6,7},{7,6},{8,9},{9,8},{10,11... | collective-permute-start | bytes 1572872 | tf_op jit(solution)/shard_map/ppermute | solution.py:298
  272.5 93.3 %collective-permute-start.1 = (bf16[512,1024]{1,0:T(8,128)(2,1)}, bf16[512,1024]{1,0:T(8,128)(2,1)}, u32[]{:S(2)}, u32[]{:S(2)}) collective-permute-start(bf16[512,1024]{1,0:T(8,128)(2,1)} %dynamic-slice_bitcast_fusion.1), channel_id=1, source_target_pairs={{0,1},{1,0},{2,3},{3,2},{4,5},{5,4},{6,7},{7,6},{8,9},{9,8},{10,11... | collective-permute-start | bytes 3145736 | tf_op jit(solution)/shard_map/ppermute | solution.py:298
  288.9 37.7 %collective-permute-start.9 = (bf16[2,2,2,64,1024]{4,3,1,0,2:T(8,128)(2,1)}, bf16[2,2,2,64,1024]{4,3,1,0,2:T(8,128)(2,1)}, u32[]{:S(2)}, u32[]{:S(2)}) collective-permute-start(bf16[2,2,2,64,1024]{4,3,1,0,2:T(8,128)(2,1)} %bitcast.205), channel_id=1, source_target_pairs={{0,2},{2,0},{4,6},{6,4},{8,10},{10,8},{12,14},{14,12},{16,18},{18,... | collective-permute-start | bytes 3145736 | tf_op jit(solution)/shard_map/ppermute | solution.py:298
  288.9 53.8 %collective-permute-start.13 = (bf16[2,2,2,64,1024]{4,3,1,0,2:T(8,128)(2,1)}, bf16[2,2,2,64,1024]{4,3,1,0,2:T(8,128)(2,1)}, u32[]{:S(2)}, u32[]{:S(2)}) collective-permute-start(bf16[2,2,2,64,1024]{4,3,1,0,2:T(8,128)(2,1)} %bitcast.204), channel_id=1, source_target_pairs={{0,2},{2,0},{4,6},{6,4},{8,10},{10,8},{12,14},{14,12},{16,18},{18,... | collective-permute-start | bytes 3145736 | tf_op jit(solution)/shard_map/ppermute | solution.py:298
  303.8 1.8 collective-permute-start.17
  305.7 7.9 %collective-permute-start.18 = (bf16[2,2,64,272]{3,2,1,0:T(8,128)(2,1)S(1)}, bf16[2,2,64,272]{3,2,1,0:T(8,128)(2,1)S(1)}, u32[]{:S(2)}, u32[]{:S(2)}) collective-permute-start(bf16[2,2,64,272]{3,2,1,0:T(8,128)(2,1)S(1)} %dynamic-slice_bitcast_fusion.9), channel_id=1, source_target_pairs={{0,4},{2,6},{4,0},{6,2},{8,12},{10,14},{12,8},{14,10},{16,20},{18,... | collective-permute-start | bytes 417800 | tf_op jit(solution)/shard_map/ppermute | solution.py:298
  313.1 25.2 %collective-permute-start.2 = (bf16[512,1024]{1,0:T(8,128)(2,1)}, bf16[512,1024]{1,0:T(8,128)(2,1)}, u32[]{:S(2)}, u32[]{:S(2)}) collective-permute-start(bf16[512,1024]{1,0:T(8,128)(2,1)} %dynamic-slice_bitcast_fusion), channel_id=1, source_target_pairs={{0,1},{1,0},{2,3},{3,2},{4,5},{5,4},{6,7},{7,6},{8,9},{9,8},{10,11... | collective-permute-start | bytes 3145736 | tf_op jit(solution)/shard_map/ppermute | solution.py:298
  313.7 7.3 %collective-permute-start.19 = (bf16[2,64,272]{2,1,0:T(8,128)(2,1)S(1)}, bf16[2,64,272]{2,1,0:T(8,128)(2,1)S(1)}, u32[]{:S(2)}, u32[]{:S(2)}) collective-permute-start(bf16[2,64,272]{2,1,0:T(8,128)(2,1)S(1)} %dynamic-slice_bitcast_fusion.13), channel_id=1, source_target_pairs={{0,16},{2,18},{4,20},{6,22},{8,24},{10,26},{12,28},{14,30},{16,0},... | collective-permute-start | bytes 208904 | tf_op jit(solution)/shard_map/ppermute | solution.py:298
  321.1 4.2 collective-permute-start.20
  325.2 21.6 %collective-permute-start.21 = (bf16[2,2,2,64,1024]{4,3,1,0,2:T(8,128)(2,1)}, bf16[2,2,2,64,1024]{4,3,1,0,2:T(8,128)(2,1)}, u32[]{:S(2)}, u32[]{:S(2)}) collective-permute-start(bf16[2,2,2,64,1024]{4,3,1,0,2:T(8,128)(2,1)} %bitcast.216), channel_id=1, source_target_pairs={{0,2},{2,0},{4,6},{6,4},{8,10},{10,8},{12,14},{14,12},{16,18},{18,... | collective-permute-start | bytes 3145736 | tf_op jit(solution)/shard_map/ppermute | solution.py:298
  330.2 43.9 %collective-permute-start.10 = (bf16[2,2,64,1024]{3,2,1,0:T(8,128)(2,1)}, bf16[2,2,64,1024]{3,2,1,0:T(8,128)(2,1)}, u32[]{:S(2)}, u32[]{:S(2)}) collective-permute-start(bf16[2,2,64,1024]{3,2,1,0:T(8,128)(2,1)} %dynamic-slice_bitcast_fusion.4), channel_id=1, source_target_pairs={{0,4},{2,6},{4,0},{6,2},{8,12},{10,14},{12,8},{14,10},{16,20},{18,... | collective-permute-start | bytes 1572872 | tf_op jit(solution)/shard_map/ppermute | solution.py:298
  342.1 4.6 %collective-permute-start.4 = (f32[1024]{0:T(1024)S(1)}, f32[1024]{0:T(1024)S(1)}, u32[]{:S(2)}, u32[]{:S(2)}) collective-permute-start(f32[1024]{0:T(1024)S(1)} %get-tuple-element.88), channel_id=1, source_target_pairs={{0,1},{1,0},{2,3},{3,2},{4,5},{5,4},{6,7},{7,6},{8,9},{9,8},{10,11... | collective-permute-start | bytes 12296 | tf_op jit(solution)/shard_map/ppermute | solution.py:298
  345.2 32.3 %collective-permute-start.14 = (bf16[2,2,64,1024]{3,2,1,0:T(8,128)(2,1)}, bf16[2,2,64,1024]{3,2,1,0:T(8,128)(2,1)}, u32[]{:S(2)}, u32[]{:S(2)}) collective-permute-start(bf16[2,2,64,1024]{3,2,1,0:T(8,128)(2,1)} %dynamic-slice_bitcast_fusion.3), channel_id=1, source_target_pairs={{0,4},{2,6},{4,0},{6,2},{8,12},{10,14},{12,8},{14,10},{16,20},{18,... | collective-permute-start | bytes 1572872 | tf_op jit(solution)/shard_map/ppermute | solution.py:298
  346.8 1.9 collective-permute-start.5
  348.7 12.4 %collective-permute-start.6 = (f32[72,128]{1,0:T(8,128)S(1)}, f32[72,128]{1,0:T(8,128)S(1)}, u32[]{:S(2)}, u32[]{:S(2)}) collective-permute-start(f32[72,128]{1,0:T(8,128)S(1)} %fusion.72), channel_id=1, source_target_pairs={{0,4},{2,6},{4,0},{6,2},{8,12},{10,14},{12,8},{14,10},{16,20},{18,... | collective-permute-start | bytes 110600 | tf_op jit(solution)/shard_map/ppermute | solution.py:298
  350.2 29.6 %collective-permute-start.22 = (bf16[2,2,64,1024]{3,2,1,0:T(8,128)(2,1)}, bf16[2,2,64,1024]{3,2,1,0:T(8,128)(2,1)}, u32[]{:S(2)}, u32[]{:S(2)}) collective-permute-start(bf16[2,2,64,1024]{3,2,1,0:T(8,128)(2,1)} %dynamic-slice_bitcast_fusion.2), channel_id=1, source_target_pairs={{0,4},{2,6},{4,0},{6,2},{8,12},{10,14},{12,8},{14,10},{16,20},{18,... | collective-permute-start | bytes 1572872 | tf_op jit(solution)/shard_map/ppermute | solution.py:298
  361.1 4.0 collective-permute-start.7
  365.1 5.2 %collective-permute-start.8 = (f32[72,128]{1,0:T(8,128)S(1)}, f32[72,128]{1,0:T(8,128)S(1)}, u32[]{:S(2)}, u32[]{:S(2)}) collective-permute-start(f32[72,128]{1,0:T(8,128)S(1)} %add.237), channel_id=1, source_target_pairs={{0,16},{2,18},{4,20},{6,22},{8,24},{10,26},{12,28},{14,30},{16,0},... | collective-permute-start | bytes 110600 | tf_op jit(solution)/shard_map/ppermute | solution.py:298
  375.4 21.9 %collective-permute-start.11 = (bf16[2,64,1024]{2,1,0:T(8,128)(2,1)S(1)}, bf16[2,64,1024]{2,1,0:T(8,128)(2,1)S(1)}, u32[]{:S(2)}, u32[]{:S(2)}) collective-permute-start(bf16[2,64,1024]{2,1,0:T(8,128)(2,1)S(1)} %dynamic-slice_bitcast_fusion.8), channel_id=1, source_target_pairs={{0,16},{2,18},{4,20},{6,22},{8,24},{10,26},{12,28},{14,30},{16,0},... | collective-permute-start | bytes 786440 | tf_op jit(solution)/shard_map/ppermute | solution.py:298
  378.8 24.3 %collective-permute-start.15 = (bf16[2,64,1024]{2,1,0:T(8,128)(2,1)S(1)}, bf16[2,64,1024]{2,1,0:T(8,128)(2,1)S(1)}, u32[]{:S(2)}, u32[]{:S(2)}) collective-permute-start(bf16[2,64,1024]{2,1,0:T(8,128)(2,1)S(1)} %dynamic-slice_bitcast_fusion.7), channel_id=1, source_target_pairs={{0,16},{2,18},{4,20},{6,22},{8,24},{10,26},{12,28},{14,30},{16,0},... | collective-permute-start | bytes 786440 | tf_op jit(solution)/shard_map/ppermute | solution.py:298
  381.1 26.3 %collective-permute-start.23 = (bf16[2,64,1024]{2,1,0:T(8,128)(2,1)S(1)}, bf16[2,64,1024]{2,1,0:T(8,128)(2,1)S(1)}, u32[]{:S(2)}, u32[]{:S(2)}) collective-permute-start(bf16[2,64,1024]{2,1,0:T(8,128)(2,1)S(1)} %dynamic-slice_bitcast_fusion.6), channel_id=1, source_target_pairs={{0,16},{2,18},{4,20},{6,22},{8,24},{10,26},{12,28},{14,30},{16,0},... | collective-permute-start | bytes 786440 | tf_op jit(solution)/shard_map/ppermute | solution.py:298
  397.4 12.7 %collective-permute-start.12 = (bf16[64,1024]{1,0:T(8,128)(2,1)S(1)}, bf16[64,1024]{1,0:T(8,128)(2,1)S(1)}, u32[]{:S(2)}, u32[]{:S(2)}) collective-permute-start(bf16[64,1024]{1,0:T(8,128)(2,1)S(1)} %dynamic-slice_bitcast_fusion.12), channel_id=1, source_target_pairs={{0,8},{2,10},{4,12},{6,14},{8,0},{10,2},{12,4},{14,6},{16,24},{18,... | collective-permute-start | bytes 393224 | tf_op jit(solution)/shard_map/ppermute | solution.py:298
  403.2 9.8 %collective-permute-start.16 = (bf16[64,1024]{1,0:T(8,128)(2,1)S(1)}, bf16[64,1024]{1,0:T(8,128)(2,1)S(1)}, u32[]{:S(2)}, u32[]{:S(2)}) collective-permute-start(bf16[64,1024]{1,0:T(8,128)(2,1)S(1)} %dynamic-slice_bitcast_fusion.11), channel_id=1, source_target_pairs={{0,8},{2,10},{4,12},{6,14},{8,0},{10,2},{12,4},{14,6},{16,24},{18,... | collective-permute-start | bytes 393224 | tf_op jit(solution)/shard_map/ppermute | solution.py:298
  407.4 8.2 %collective-permute-start.24 = (bf16[64,1024]{1,0:T(8,128)(2,1)S(1)}, bf16[64,1024]{1,0:T(8,128)(2,1)S(1)}, u32[]{:S(2)}, u32[]{:S(2)}) collective-permute-start(bf16[64,1024]{1,0:T(8,128)(2,1)S(1)} %dynamic-slice_bitcast_fusion.10), channel_id=1, source_target_pairs={{0,8},{2,10},{4,12},{6,14},{8,0},{10,2},{12,4},{14,6},{16,24},{18,... | collective-permute-start | bytes 393224 | tf_op jit(solution)/shard_map/ppermute | solution.py:298
  (34 other events, 232.2 us)
Sparse Core Ops, SparseCore 0:
  11.5 35.8 all-gather.6
  49.5 41.4 all-gather.10
  93.1 40.1 all-gather.8
  134.7 31.8 all-gather.14
  168.7 41.3 all-gather.12
